TPU v7x, 256 devices: a whole 4x4x8 slice. The times are simulated.
256 devices in a mesh: dp: 32 (over z, x), ctx: 2 (over core), tp: 4 (over y).
Axes of the slice: x: 4, y: 4, z: 8, core: 2. Of those that a mesh axis runs over, the one named last changes fastest.
Arguments:
- head_inputs: bfloat16 [32768, 8192], P(('dp', 'ctx'), 'tp'), may hold values from -6 to 6
- write_vecs: bfloat16 [32768, 1024], P(('dp', 'ctx'), 'tp'), may hold values from -6 to 6
- read_vecs: bfloat16 [32768, 1024], P(('dp', 'ctx'), 'tp'), may hold values from -6 to 6
- step_raw: bfloat16 [32768, 128], P(('dp', 'ctx'), 'tp'), may hold values from -8 to 5
- decay_log: float32 [128], P('tp'), may hold values from -5 to 2.5
- step_bias: float32 [128], P('tp'), may hold values from -0.5 to 0.5
- skip_gain: float32 [128], P('tp'), may hold values from 0.5 to 1.5
- out_cotangent: bfloat16 [32768, 8192], P(('dp', 'ctx'), 'tp'), may hold values from -6 to 6
- rollout_lengths: int32 [32, 3], P('dp'), may hold values from 1 to 512, 1024 in all within a row
- plan_place: int32 [32768], P(('dp', 'ctx')), may hold values from 0 to 32767, as said below
- plan_anchor: int32 [32768], P(('dp', 'ctx')), may hold values from 0 to 32767, as said below
Outputs:
- layer_out: bfloat16 [32768, 8192], P(('dp', 'ctx'), 'tp')
- grad_inputs: bfloat16 [32768, 8192], P(('dp', 'ctx'), 'tp')
- grad_write: bfloat16 [32768, 1024], P(('dp', 'ctx'), 'tp')
- grad_read: bfloat16 [32768, 1024], P(('dp', 'ctx'), 'tp')
- grad_step: bfloat16 [32768, 128], P(('dp', 'ctx'), 'tp')
- param_grads: float32 [3, 128], P(None, 'tp')
Inputs may be any that keep to these rules, and one draw needn't show every extreme that they name: `plan_place`: all values distinct; the rows that one generator device sends to one device number at most 16, exactly 16 for some pairs; every device receives 512 rows; the lists of counts from each generator device to the 64 devices are rearrangements of one list. `plan_anchor`: the inverse of plan_place.
All inputs are finite; a program needn't handle non-finite values.
Results may differ from a plain program's by a relative error of at most 0.0039.
Values may be sent and summed in bfloat16 or wider, within the bound.
A program may use at most 128 MiB of HBM per device.

v0:
```python
import math

import jax
import jax.numpy as jnp
from jax import lax
from jax.sharding import PartitionSpec as P

HEAD = 64
STATE = 256
BLOCK = 256


PRECISE = lax.Precision.HIGHEST


def prefix(x, axis, combine, identity, reverse):
    peers, here = (lax.axis_size(axis), lax.axis_index(axis))
    everything = jax.tree.map(lambda part: lax.all_gather(part, axis), x)
    start = jax.tree.map(
        lambda part, zero: jnp.broadcast_to(jnp.asarray(zero, part.dtype), part.shape), x, identity
    )

    def hop(k, before):
        at = peers - 1 - k if reverse else k
        reached = at > here if reverse else at < here
        new = combine(before, jax.tree.map(lambda part: part[at], everything))
        return jax.tree.map(lambda a, b: jnp.where(reached, a, b), new, before)

    return lax.fori_loop(0, peers, hop, start)


def block_step(carry_state, pieces, decay_rate, gain_vals):
    head_rows, write_rows, read_rows, step_size, starts = pieces
    row_count = head_rows.shape[0]
    attention_unit_number = step_size.shape[1]
    group_count = write_rows.shape[1] // STATE
    per_group = attention_unit_number // group_count
    head_vals = head_rows.astype(jnp.float32).reshape(row_count, group_count, per_group, HEAD)
    write_grp = write_rows.astype(jnp.float32).reshape(row_count, group_count, STATE)
    read_grp = read_rows.astype(jnp.float32).reshape(row_count, group_count, STATE)
    running = jnp.cumsum(step_size * decay_rate[None, :], axis=0)
    segment = jnp.cumsum(starts)
    row_index = jnp.arange(row_count)
    same_seg = (segment[:, None] == segment[None, :]) & (row_index[:, None] >= row_index[None, :])
    running_heads = running.T
    gaps = running_heads[:, :, None] - running_heads[:, None, :]
    decay_mat = jnp.where(same_seg[None], jnp.exp(jnp.where(same_seg[None], gaps, 0.0)), 0.0)
    intersection = jnp.einsum("tgn,sgn->gts", read_grp, write_grp, precision=PRECISE)
    scores = (
        intersection[:, None]
        * decay_mat.reshape(group_count, per_group, row_count, row_count)
        * step_size.T.reshape(group_count, per_group, 1, row_count)
    )
    inner_part = jnp.einsum("gjts,sgjp->tgjp", scores, head_vals, precision=PRECISE)
    entering = jnp.exp(running) * (segment == 0)[:, None]
    state_four = carry_state.reshape(group_count, per_group, HEAD, STATE)
    carried = jnp.einsum("tgn,gjpn->tgjp", read_grp, state_four, precision=PRECISE)
    output = (
        inner_part
        + entering.reshape(row_count, group_count, per_group, 1) * carried
        + gain_vals.reshape(1, group_count, per_group, 1) * head_vals
    )
    leaving = jnp.exp(running[-1][None, :] - running) * (segment == segment[-1])[:, None]
    keeping = jnp.exp(running[-1]) * (segment[-1] == 0)
    weighted = (leaving * step_size).reshape(row_count, group_count, per_group, 1) * head_vals
    fresh_state = jnp.einsum("sgjp,sgn->gjpn", weighted, write_grp, precision=PRECISE)
    new_state = fresh_state + keeping.reshape(group_count, per_group, 1, 1) * state_four
    return (
        new_state.reshape(attention_unit_number, HEAD, STATE),
        output.reshape(row_count, attention_unit_number * HEAD),
    )


def block_state(carry_state, pieces, decay_rate):
    head_rows, write_rows, step_size, starts = pieces
    row_count = head_rows.shape[0]
    attention_unit_number = step_size.shape[1]
    group_count = write_rows.shape[1] // STATE
    per_group = attention_unit_number // group_count
    head_vals = head_rows.astype(jnp.float32).reshape(row_count, group_count, per_group, HEAD)
    write_grp = write_rows.astype(jnp.float32).reshape(row_count, group_count, STATE)
    running = jnp.cumsum(step_size * decay_rate[None, :], axis=0)
    segment = jnp.cumsum(starts)
    leaving = jnp.exp(running[-1][None, :] - running) * (segment == segment[-1])[:, None]
    keeping = jnp.exp(running[-1]) * (segment[-1] == 0)
    weighted = (leaving * step_size).reshape(row_count, group_count, per_group, 1) * head_vals
    fresh_state = jnp.einsum("sgjp,sgn->gjpn", weighted, write_grp, precision=PRECISE)
    state_four = carry_state.reshape(group_count, per_group, HEAD, STATE)
    new_state = fresh_state + keeping.reshape(group_count, per_group, 1, 1) * state_four
    return (new_state.reshape(attention_unit_number, HEAD, STATE), None)


def run_blocks(
    head_rows,
    write_rows,
    read_rows,
    step_rows,
    log_decay,
    bias_vals,
    gain_vals,
    starts,
    first_state,
):
    row_count = head_rows.shape[0]
    block_count = row_count // BLOCK
    step_size = jax.nn.softplus(step_rows.astype(jnp.float32) + bias_vals[None, :])
    decay_rate = -jnp.exp(log_decay)

    def advance(carry_state, pieces):
        return jax.checkpoint(block_step)(carry_state, pieces, decay_rate, gain_vals)

    pieces = (
        head_rows.reshape(block_count, BLOCK, -1),
        write_rows.reshape(block_count, BLOCK, -1),
        read_rows.reshape(block_count, BLOCK, -1),
        step_size.reshape(block_count, BLOCK, -1),
        starts.reshape(block_count, BLOCK),
    )
    final_state, outputs = lax.scan(advance, first_state, pieces)
    return (outputs.reshape(row_count, -1), final_state)


def combine(earlier_part, later_part):
    return (
        earlier_part[0] * later_part[0],
        later_part[1] + later_part[0][:, None, None] * earlier_part[1],
    )


def per_device(
    head_inputs,
    write_vecs,
    read_vecs,
    step_raw,
    decay_log,
    step_bias,
    skip_gain,
    out_cotangent,
    rollout_lengths,
    plan_place,
    plan_anchor,
):
    tok_rows = head_inputs.shape[0]
    dp_count = lax.axis_size("dp")
    ctx_count = lax.axis_size("ctx")
    gen_count = dp_count * ctx_count
    capacity = 2 * tok_rows // gen_count
    slot_count = gen_count * capacity
    device_ids = jnp.arange(gen_count, dtype=jnp.int32)
    target = plan_place // tok_rows
    matches = (target[:, None] == device_ids[None, :]).astype(jnp.int32)
    before = jnp.cumsum(matches, axis=0) - matches
    send_slot = target * capacity + jnp.sum(before * matches, axis=1)
    source = plan_anchor // tok_rows
    source_row = plan_anchor % tok_rows
    earlier_peer = (source[:, None] == source[None, :]) & (
        source_row[None, :] < source_row[:, None]
    )
    take_slot = source * capacity + jnp.sum(earlier_peer.astype(jnp.int32), axis=1)

    def spread_width(values, slots):
        return jnp.zeros((slot_count, values.shape[1]), values.dtype).at[slots].set(values)

    send_inputs = spread_width(head_inputs, send_slot)
    send_writes = spread_width(write_vecs, send_slot)
    send_reads = spread_width(read_vecs, send_slot)
    send_steps = spread_width(step_raw, send_slot)
    arrived = (
        lax.all_to_all(send_inputs, ("dp", "ctx"), split_axis=0, concat_axis=0, tiled=True),
        lax.all_to_all(send_writes, ("dp", "ctx"), split_axis=0, concat_axis=0, tiled=True),
        lax.all_to_all(send_reads, ("dp", "ctx"), split_axis=0, concat_axis=0, tiled=True),
        lax.all_to_all(send_steps, ("dp", "ctx"), split_axis=0, concat_axis=0, tiled=True),
    )
    packed_inputs = arrived[0][take_slot]
    packed_writes = arrived[1][take_slot]
    packed_reads = arrived[2][take_slot]
    packed_steps = arrived[3][take_slot]
    ctx_index = lax.axis_index("ctx")
    bounds = jnp.cumsum(rollout_lengths[0]) - rollout_lengths[0]
    position = ctx_index * tok_rows + jnp.arange(tok_rows, dtype=jnp.int32)
    starts = jnp.any(position[:, None] == bounds[None, :], axis=1).astype(jnp.int32)
    attention_unit_number = packed_steps.shape[1]
    group_count = packed_writes.shape[1] // STATE
    per_group = attention_unit_number // group_count
    block_count = tok_rows // BLOCK
    step_size = jax.nn.softplus(packed_steps.astype(jnp.float32) + step_bias[None, :])
    decay_rate = -jnp.exp(decay_log)
    zero_state = jnp.zeros((attention_unit_number, HEAD, STATE), jnp.float32)

    def advance_state(carry_state, pieces):
        return block_state(carry_state, pieces, decay_rate)

    local_state, _ = lax.scan(
        advance_state,
        zero_state,
        (
            packed_inputs.reshape(block_count, BLOCK, -1),
            packed_writes.reshape(block_count, BLOCK, -1),
            step_size.reshape(block_count, BLOCK, -1),
            starts.reshape(block_count, BLOCK),
        ),
    )
    running_all = jnp.cumsum(step_size * decay_rate[None, :], axis=0)
    through = jnp.exp(running_all[-1]) * (jnp.sum(starts) == 0)
    neutral_couple = (jnp.ones((attention_unit_number,), jnp.float32), zero_state)
    _, state_in = prefix((through, local_state), "ctx", combine, neutral_couple, False)
    entering = jnp.exp(running_all) * (jnp.cumsum(starts) == 0)[:, None]
    cot_heads = out_cotangent.astype(jnp.float32).reshape(tok_rows, group_count, per_group, HEAD)
    read_heads = packed_reads.astype(jnp.float32).reshape(tok_rows, group_count, STATE)
    own_grad = jnp.einsum(
        "tgjp,tgn->gjpn",
        entering.reshape(tok_rows, group_count, per_group, 1) * cot_heads,
        read_heads,
        precision=PRECISE,
    ).reshape(attention_unit_number, HEAD, STATE)
    _, state_grad = prefix((through, own_grad), "ctx", combine, neutral_couple, True)

    def forward(head_arg, write_arg, read_arg, step_arg, decay_arg, bias_arg, gain_arg):
        return run_blocks(
            head_arg, write_arg, read_arg, step_arg, decay_arg, bias_arg, gain_arg, starts, state_in
        )

    (layer_out, leaving_state), pullback = jax.vjp(
        forward,
        packed_inputs,
        packed_writes,
        packed_reads,
        packed_steps,
        decay_log,
        step_bias,
        skip_gain,
    )
    gradients = pullback((out_cotangent.astype(jnp.float32), state_grad))
    back_inputs = spread_width(gradients[0], take_slot)
    back_writes = spread_width(gradients[1], take_slot)
    back_reads = spread_width(gradients[2], take_slot)
    back_steps = spread_width(gradients[3], take_slot)
    returning = (
        lax.all_to_all(back_inputs, ("dp", "ctx"), split_axis=0, concat_axis=0, tiled=True),
        lax.all_to_all(back_writes, ("dp", "ctx"), split_axis=0, concat_axis=0, tiled=True),
        lax.all_to_all(back_reads, ("dp", "ctx"), split_axis=0, concat_axis=0, tiled=True),
        lax.all_to_all(back_steps, ("dp", "ctx"), split_axis=0, concat_axis=0, tiled=True),
    )
    local_params = jnp.stack([gradients[4], gradients[5], gradients[6]])
    total_params = lax.psum(local_params, ("dp", "ctx"))
    param_grads = total_params * (1.0 / math.sqrt(tok_rows * gen_count * HEAD))
    return (
        layer_out.astype(jnp.bfloat16),
        returning[0][send_slot],
        returning[1][send_slot],
        returning[2][send_slot],
        returning[3][send_slot],
        param_grads,
    )


def solution(mesh):
    placed = (
        P(("dp", "ctx"), "tp"),
        P(("dp", "ctx"), "tp"),
        P(("dp", "ctx"), "tp"),
        P(("dp", "ctx"), "tp"),
        P("tp"),
        P("tp"),
        P("tp"),
        P(("dp", "ctx"), "tp"),
        P("dp", None),
        P(("dp", "ctx")),
        P(("dp", "ctx")),
    )
    return jax.shard_map(
        per_device,
        mesh=mesh,
        in_specs=placed,
        out_specs=(
            P(("dp", "ctx"), "tp"),
            P(("dp", "ctx"), "tp"),
            P(("dp", "ctx"), "tp"),
            P(("dp", "ctx"), "tp"),
            P(("dp", "ctx"), "tp"),
            P(None, "tp"),
        ),
        check_vma=False,
    )
```

profile of v0, /device:TPU:1, one launch (start us, length us, event | category | flops | bytes accessed | tf_op | source)
XLA Modules:
  0.0 797.6 jit_solution(9924266451041473849)
XLA Ops:
  14.4 13.0 %all-to-all-start = ((bf16[64,2,256]{2,1,0:T(2,128)(2,1)}), bf16[64,2,256]{2,1,0:T(2,128)(2,1)S(1)}, u32[]{:S(2)}, u32[]{:S(2)}) async-start(bf16[64,2,256]{2,1,0:T(2,128)(2,1)} %reshape.1352), calls=%async_computation | async-start | bytes 131072 | tf_op jit(solution)/shard_map/all_to_all | solution.py:172
  27.4 3.5 scatter_custom_fusion.2
  30.9 6.6 all-to-all-done
  37.5 4.5 all-to-all-start.2
  42.0 3.5 scatter_custom_fusion.3
  45.5 14.3 %all-to-all-done.2 = bf16[64,16,256]{2,1,0:T(8,128)(2,1)S(1)} async-done(((bf16[64,16,256]{2,1,0:T(8,128)(2,1)}), bf16[64,16,256]{2,1,0:T(8,128)(2,1)S(1)}, u32[]{:S(2)}, u32[]{:S(2)}) %all-to-all-start.2) | async-done | bytes 524320 | tf_op jit(solution)/shard_map/all_to_all | solution.py:170
  59.8 6.3 all-to-all-start.3
  66.1 7.3 scatter_custom_fusion.1
  73.4 10.3 %all-to-all-done.3 = bf16[64,16,256]{2,1,0:T(8,128)(2,1)S(1)} async-done(((bf16[64,16,256]{2,1,0:T(8,128)(2,1)}), bf16[64,16,256]{2,1,0:T(8,128)(2,1)S(1)}, u32[]{:S(2)}, u32[]{:S(2)}) %all-to-all-start.3) | async-done | bytes 524320 | tf_op jit(solution)/shard_map/all_to_all | solution.py:171
  83.7 6.0 all-to-all-start.1
  91.3 2.9 copy.220
  111.5 5.6 fusion.105
  117.2 67.0 %all-to-all-done.1 = bf16[64,16,2048]{2,1,0:T(8,128)(2,1)} async-done(((bf16[64,16,2048]{2,1,0:T(8,128)(2,1)}), bf16[64,16,2048]{2,1,0:T(8,128)(2,1)}, u32[]{:S(2)}, u32[]{:S(2)}) %all-to-all-start.1) | async-done | bytes 4194336 | tf_op jit(solution)/shard_map/all_to_all | solution.py:169
  184.2 7.1 gather_fusion.1
  193.8 20.4 %while.86 = (s32[]{:T(128)}, f32[32,64,256]{2,1,0:T(8,128)}, f32[2,256,32]{1,2,0:T(8,128)S(1)}, f32[32]{0:T(128)}, s32[2,256]{1,0:T(2,128)}, /*index=5*/bf16[2,2...) while((s32[]{:T(128)}, f32[32,64,256]{2,1,0:T(8,128)}, ...), condition=%wide.region_17.18_spmd.clone, body=%wide.region_12.17_spmd.clone.sunk | while | flops 1614357120 | bytes 9908969 | solution.py:193
  200.3 3.3 fusion.222
  210.2 4.1 fusion.222
  214.3 4.1 copy.221
  220.0 4.2 all-gather.2
  224.2 4.8 while.88
  229.1 3.1 all-gather.6.cloned.1.call-done
  232.1 7.1 while.87
  232.1 3.2 fusion.223
  235.4 3.9 fusion.223
  239.3 56.8 %while.85 = (s32[]{:T(128)}, f32[32,64,256]{2,1,0:T(8,128)}, bf16[2,256,2048]{1,2,0:T(8,128)(2,1)}, f32[2,32,64,256]{3,2,1,0:T(8,128)}, f32[2,256,32]{1,2,0:T(8,...) while((s32[]{:T(128)}, f32[32,64,256]{2,1,0:T(8,128)}, ...), condition=%wide.region_26.27_spmd.clone, body=%wide.region_21.26_spmd.clone.sunk | while | flops 4882449408 | bytes 53135704 | solution.py:119
  250.0 8.2 %fusion.218 = bf16[256,1,32,64]{0,3,2,1:T(8,128)(2,1)S(1)} fusion(f32[256,32,64]{0,2,1:T(8,128)S(1)} %fusion.215, bf16[256,32,64]{0,2,1:T(8,128)(2,1)S(1)} %bitcast.613, f32[32,256]{1,0:T(8,128)S(1)} %dynamic-slice_bitcast_fusion.15, f32[32,256]{1,0:T(8,128)S(1)} %get-tuple-element.1606, f32[256,256]{1,0:T(8,128)S(1)} %fusion.216, ...), kind=kOutput, calls=%fused_computation.38.clone.1 | convolution fusion | flops 1624244224 | bytes 5668992 | tf_op jit(solution)/shard_map/jvp()/while/body/eval_jaxpr/gjts,sgjp->tgjp/dot_general | solution.py:54
  260.3 3.3 bitcast_dynamic-update-slice_fusion.4
  263.6 4.1 multiply_add_fusion.4
  278.4 8.2 %fusion.218 = bf16[256,1,32,64]{0,3,2,1:T(8,128)(2,1)S(1)} fusion(f32[256,32,64]{0,2,1:T(8,128)S(1)} %fusion.215, bf16[256,32,64]{0,2,1:T(8,128)(2,1)S(1)} %bitcast.613, f32[32,256]{1,0:T(8,128)S(1)} %dynamic-slice_bitcast_fusion.15, f32[32,256]{1,0:T(8,128)S(1)} %get-tuple-element.1606, f32[256,256]{1,0:T(8,128)S(1)} %fusion.216, ...), kind=kOutput, calls=%fused_computation.38.clone.1 | convolution fusion | flops 1624244224 | bytes 5668992 | tf_op jit(solution)/shard_map/jvp()/while/body/eval_jaxpr/gjts,sgjp->tgjp/dot_general | solution.py:54
  288.6 3.3 bitcast_dynamic-update-slice_fusion.4
  291.9 4.1 multiply_add_fusion.4
  299.8 189.8 %while.89 = (s32[]{:T(128)}, f32[32]{0:T(128)}, f32[32]{0:T(128)}, f32[32,64,256]{2,1,0:T(8,128)S(1)}, bf16[2,256,2048]{2,1,0:T(8,128)(2,1)}, /*index=5*/bf16[2,...) while((s32[]{:T(128)}, f32[32]{0:T(128)}, f32[32]{0:T(128)}, ...), condition=%wide.region_49.50_spmd.clone, body=%wide.region_31.49_spmd.clone.sunk | while | flops 11765654528 | bytes 104165248 | solution.py:119
  301.3 3.1 constant_dynamic-slice_fusion.13
  306.4 3.3 dynamic-slice_bitcast_fusion.18
  311.4 4.6 fusion.248
  320.0 3.1 multiply_reduce_fusion.5
  331.0 3.3 fusion.247
  339.1 11.7 %fusion.246 = (f32[32,256]{1,0:T(8,128)}, f32[32,256]{1,0:T(8,128)}, f32[32,256]{1,0:T(8,128)}, f32[256,256]{1,0:T(8,128)}) fusion(f32[32,256]{1,0:T(8,128)} %copy_bitcast_fusion.11, f32[32,256]{1,0:T(8,128)} %copy.292, f32[256,256]{1,0:T(8,128)} %fusion.244, pred[256,256]{1,0:T(8,128)(4,1)} %fusion.245, f32[32,64,256]{2,1,0:T(8,128)S(1)} %bitcast.598, ...), kind=kOutput, calls=%fused_computation.105.clone.1 | convolution fusion | flops 1641979904 | bytes 3899392 | tf_op jit(solution)/shard_map/transpose(jvp())/while/body/eval_jaxpr/checkpoint/gjts,sgjp->tgjp/dot_general | solution.py:54
  357.3 5.1 fusion.254
  365.0 10.0 %fusion.252 = bf16[256,1,32,64]{0,3,2,1:T(8,128)(2,1)} fusion(f32[32,64,256]{2,1,0:T(8,128)} %get-tuple-element.1667, f32[256,1,32,64]{0,3,2,1:T(8,128)S(1)} %bitcast.601, f32[32,64,256]{2,1,0:T(8,128)S(1)} %bitcast.600, f32[32,256]{1,0:T(8,128)} %copy_bitcast_fusion.11, f32[32,256]{1,0:T(8,128)} %copy.292, f32[256,256]{1,0:T(8,128)} %fusion.244, ...), kind=kOutput, calls=%fused_computation.113.clone.1 | convolution fusion | flops 1623719936 | bytes 7766144 | tf_op jit(solution)/shard_map/transpose(jvp())/while/body/eval_jaxpr/checkpoint/gjts,sgjp->tgjp/dot_general | solution.py:54
  380.4 5.1 fusion.253
  385.5 4.1 multiply_add_fusion.5
  396.0 3.1 constant_dynamic-slice_fusion.13
  401.0 3.3 dynamic-slice_bitcast_fusion.18
  406.0 4.6 fusion.248
  414.7 3.1 multiply_reduce_fusion.5
  425.7 3.3 fusion.247
  433.7 11.7 %fusion.246 = (f32[32,256]{1,0:T(8,128)}, f32[32,256]{1,0:T(8,128)}, f32[32,256]{1,0:T(8,128)}, f32[256,256]{1,0:T(8,128)}) fusion(f32[32,256]{1,0:T(8,128)} %copy_bitcast_fusion.11, f32[32,256]{1,0:T(8,128)} %copy.292, f32[256,256]{1,0:T(8,128)} %fusion.244, pred[256,256]{1,0:T(8,128)(4,1)} %fusion.245, f32[32,64,256]{2,1,0:T(8,128)S(1)} %bitcast.598, ...), kind=kOutput, calls=%fused_computation.105.clone.1 | convolution fusion | flops 1641979904 | bytes 3899392 | tf_op jit(solution)/shard_map/transpose(jvp())/while/body/eval_jaxpr/checkpoint/gjts,sgjp->tgjp/dot_general | solution.py:54
  451.9 5.1 fusion.254
  459.7 10.0 %fusion.252 = bf16[256,1,32,64]{0,3,2,1:T(8,128)(2,1)} fusion(f32[32,64,256]{2,1,0:T(8,128)} %get-tuple-element.1667, f32[256,1,32,64]{0,3,2,1:T(8,128)S(1)} %bitcast.601, f32[32,64,256]{2,1,0:T(8,128)S(1)} %bitcast.600, f32[32,256]{1,0:T(8,128)} %copy_bitcast_fusion.11, f32[32,256]{1,0:T(8,128)} %copy.292, f32[256,256]{1,0:T(8,128)} %fusion.244, ...), kind=kOutput, calls=%fused_computation.113.clone.1 | convolution fusion | flops 1623719936 | bytes 7766144 | tf_op jit(solution)/shard_map/transpose(jvp())/while/body/eval_jaxpr/checkpoint/gjts,sgjp->tgjp/dot_general | solution.py:54
  475.0 5.1 fusion.253
  480.2 4.1 multiply_add_fusion.5
  493.7 9.9 %all-to-all-start.7 = ((bf16[64,2,256]{2,1,0:T(2,128)(2,1)}), bf16[64,2,256]{2,1,0:T(2,128)(2,1)S(1)}, u32[]{:S(2)}, u32[]{:S(2)}) async-start(bf16[64,2,256]{2,1,0:T(2,128)(2,1)} %reshape.1354), calls=%async_computation.7 | async-start | bytes 131072 | tf_op jit(solution)/shard_map/all_to_all | solution.py:242
  503.6 3.5 scatter_custom_fusion.5
  507.1 6.6 all-to-all-done.7
  514.3 4.5 all-to-all-start.5
  518.8 3.5 scatter_custom_fusion.6
  522.3 14.3 %all-to-all-done.5 = bf16[64,16,256]{2,1,0:T(8,128)(2,1)S(1)} async-done(((bf16[64,16,256]{2,1,0:T(8,128)(2,1)}), bf16[64,16,256]{2,1,0:T(8,128)(2,1)S(1)}, u32[]{:S(2)}, u32[]{:S(2)}) %all-to-all-start.5) | async-done | bytes 524320 | tf_op jit(solution)/shard_map/all_to_all | solution.py:240
  536.6 6.0 all-to-all-start.6
  542.6 7.2 scatter_custom_fusion.4
  549.9 10.4 %all-to-all-done.6 = bf16[64,16,256]{2,1,0:T(8,128)(2,1)S(1)} async-done(((bf16[64,16,256]{2,1,0:T(8,128)(2,1)}), bf16[64,16,256]{2,1,0:T(8,128)(2,1)S(1)}, u32[]{:S(2)}, u32[]{:S(2)}) %all-to-all-start.6) | async-done | bytes 524320 | tf_op jit(solution)/shard_map/all_to_all | solution.py:241
  560.2 6.0 all-to-all-start.4
  569.7 204.0 %psum.7 = f32[3,32]{1,0:T(4,128)S(1)} all-reduce(f32[3,32]{1,0:T(4,128)S(1)} %pad_maximum_fusion), channel_id=1, replica_groups=mesh['dp'=32,'ctx'=2,'tp'=4] {'dp','ctx'}, use_global_device_ids=true, to_apply=%region_55.56 | all-reduce | flops 96 | bytes 768 | tf_op jit(solution)/shard_map/psum | solution.py:245
  782.6 8.0 gather_fusion.4
  (413 shorter events, 170.9 us)
Async XLA Ops:
  10.9 62.5 %copy-start.36 = (s32[512]{0:T(512)}, s32[512]{0:T(512)S(1)}, u32[]{:S(2)}) copy-start(s32[512]{0:T(512)S(1)} %compare_select_fusion.8) | copy-start | bytes 6148
  14.4 23.1 %all-to-all-start = ((bf16[64,2,256]{2,1,0:T(2,128)(2,1)}), bf16[64,2,256]{2,1,0:T(2,128)(2,1)S(1)}, u32[]{:S(2)}, u32[]{:S(2)}) async-start(bf16[64,2,256]{2,1,0:T(2,128)(2,1)} %reshape.1352), calls=%async_computation | async-start | bytes 131072 | tf_op jit(solution)/shard_map/all_to_all | solution.py:172
  37.5 22.3 %all-to-all-start.2 = ((bf16[64,16,256]{2,1,0:T(8,128)(2,1)}), bf16[64,16,256]{2,1,0:T(8,128)(2,1)S(1)}, u32[]{:S(2)}, u32[]{:S(2)}) async-start(bf16[64,16,256]{2,1,0:T(8,128)(2,1)} %bitcast.9), calls=%async_computation.2 | async-start | bytes 1048576 | tf_op jit(solution)/shard_map/all_to_all | solution.py:170
  59.8 23.9 %all-to-all-start.3 = ((bf16[64,16,256]{2,1,0:T(8,128)(2,1)}), bf16[64,16,256]{2,1,0:T(8,128)(2,1)S(1)}, u32[]{:S(2)}, u32[]{:S(2)}) async-start(bf16[64,16,256]{2,1,0:T(8,128)(2,1)} %bitcast.18), calls=%async_computation.3 | async-start | bytes 1048576 | tf_op jit(solution)/shard_map/all_to_all | solution.py:171
  83.7 6.3 copy-start.42
  83.7 100.5 %all-to-all-start.1 = ((bf16[64,16,2048]{2,1,0:T(8,128)(2,1)}), bf16[64,16,2048]{2,1,0:T(8,128)(2,1)}, u32[]{:S(2)}, u32[]{:S(2)}) async-start(bf16[64,16,2048]{2,1,0:T(8,128)(2,1)} %bitcast.619), calls=%async_computation.1 | async-start | bytes 8388608 | tf_op jit(solution)/shard_map/all_to_all | solution.py:169
  89.8 134.5 %all-gather.8.cloned.1.call-start = ((), (), s32[]{:S(2)}) async-start(), calls=%async_computation.9 | async-start | bytes 6291456 | tf_op jit(solution)/shard_map/all_gather | solution.py:18
  90.3 3.9 copy-start.40
  91.3 2.9 copy-start.39
  91.3 4.3 copy-start.43
  91.3 6.5 copy-start.34
  94.2 12.2 %copy-start.9 = (bf16[512,2048]{0,1:T(8,128)(2,1)}, bf16[512,2048]{0,1:T(8,128)(2,1)S(1)}, u32[]{:S(2)}) copy-start(bf16[512,2048]{0,1:T(8,128)(2,1)S(1)} %copy.220) | copy-start | bytes 6291460
  97.8 8.6 %copy-start.13 = (bf16[512,32]{1,0:T(8,128)(2,1)}, bf16[512,32]{1,0:T(8,128)(2,1)S(1)}, u32[]{:S(2)}) copy-start(bf16[512,32]{1,0:T(8,128)(2,1)S(1)} %gather_fusion) | copy-start | bytes 98308
  117.1 115.0 %all-gather.6.cloned.1.call-start = ((), (), s32[]{:S(2)}) async-start(), calls=%async_computation.8 | async-start | bytes 6291456 | tf_op jit(solution)/shard_map/all_gather | solution.py:18
  214.3 4.1 copy-start.41
  250.0 8.2 %copy-start.18 = (bf16[2,256,2048]{1,2,0:T(8,128)(2,1)S(1)}, bf16[2,256,2048]{1,2,0:T(8,128)(2,1)}, u32[]{:S(2)}) copy-start(bf16[2,256,2048]{1,2,0:T(8,128)(2,1)} %get-tuple-element.1739) | copy-start | bytes 6291460 | tf_op jit(solution)/shard_map/jvp()/while
  260.3 3.3 copy-start.2
  278.4 8.2 %copy-start.18 = (bf16[2,256,2048]{1,2,0:T(8,128)(2,1)S(1)}, bf16[2,256,2048]{1,2,0:T(8,128)(2,1)}, u32[]{:S(2)}) copy-start(bf16[2,256,2048]{1,2,0:T(8,128)(2,1)} %get-tuple-element.1739) | copy-start | bytes 6291460 | tf_op jit(solution)/shard_map/jvp()/while
  288.6 3.3 copy-start.2
  301.2 10.1 %copy-start.5 = (bf16[256,256]{1,0:T(8,128)(2,1)}, bf16[256,256]{1,0:T(8,128)(2,1)S(1)}, u32[]{:S(2)}) copy-start(bf16[256,256]{1,0:T(8,128)(2,1)S(1)} %get-tuple-element.1649) | copy-start | bytes 393220 | tf_op jit(solution)/shard_map/transpose(jvp())/while
  306.4 3.3 copy-start.3
  339.1 14.7 %copy-start.27 = (f32[256]{0:T(256)S(1)}, f32[256]{0:T(256)}, u32[]{:S(2)}) copy-start(f32[256]{0:T(256)} %get-tuple-element.1645) | copy-start | bytes 3076 | tf_op jit(solution)/shard_map/transpose(jvp())/while
  357.3 5.1 copy-start.6
  357.3 5.2 copy-start.7
  357.3 5.2 copy-start.25
  377.3 2.7 copy-start.12
  380.4 5.1 copy-start.11
  385.5 4.3 copy-start.23
  385.5 4.5 copy-start.28
  385.5 4.5 copy-start.10
  385.5 7.4 copy-start.21
  385.5 7.5 copy-start.4
  385.5 8.3 %copy-start.15 = (f32[2,256,32]{2,1,0:T(8,128)S(1)}, f32[2,256,32]{2,1,0:T(8,128)}, u32[]{:S(2)}) copy-start(f32[2,256,32]{2,1,0:T(8,128)} %get-tuple-element.1816) | copy-start | bytes 196612 | tf_op jit(solution)/shard_map/transpose(jvp())/while
  389.6 4.2 copy-start.31
  389.6 4.9 copy-start.1
  389.8 4.1 copy-start.24
  390.0 3.9 copy-start.29
  395.9 10.2 %copy-start.5 = (bf16[256,256]{1,0:T(8,128)(2,1)}, bf16[256,256]{1,0:T(8,128)(2,1)S(1)}, u32[]{:S(2)}) copy-start(bf16[256,256]{1,0:T(8,128)(2,1)S(1)} %get-tuple-element.1649) | copy-start | bytes 393220 | tf_op jit(solution)/shard_map/transpose(jvp())/while
  401.0 3.3 copy-start.3
  433.7 14.7 %copy-start.27 = (f32[256]{0:T(256)S(1)}, f32[256]{0:T(256)}, u32[]{:S(2)}) copy-start(f32[256]{0:T(256)} %get-tuple-element.1645) | copy-start | bytes 3076 | tf_op jit(solution)/shard_map/transpose(jvp())/while
  451.9 5.1 copy-start.6
  451.9 5.2 copy-start.7
  451.9 5.2 copy-start.25
  472.0 2.7 copy-start.12
  475.0 5.1 copy-start.11
  480.1 4.3 copy-start.23
  480.1 4.5 copy-start.28
  480.2 4.5 copy-start.10
  480.2 7.4 copy-start.21
  480.2 7.5 copy-start.4
  480.2 8.3 %copy-start.15 = (f32[2,256,32]{2,1,0:T(8,128)S(1)}, f32[2,256,32]{2,1,0:T(8,128)}, u32[]{:S(2)}) copy-start(f32[2,256,32]{2,1,0:T(8,128)} %get-tuple-element.1816) | copy-start | bytes 196612 | tf_op jit(solution)/shard_map/transpose(jvp())/while
  484.3 4.2 copy-start.31
  484.3 4.9 copy-start.1
  484.4 4.1 copy-start.24
  484.7 3.9 copy-start.29
  493.7 20.0 %all-to-all-start.7 = ((bf16[64,2,256]{2,1,0:T(2,128)(2,1)}), bf16[64,2,256]{2,1,0:T(2,128)(2,1)S(1)}, u32[]{:S(2)}, u32[]{:S(2)}) async-start(bf16[64,2,256]{2,1,0:T(2,128)(2,1)} %reshape.1354), calls=%async_computation.7 | async-start | bytes 131072 | tf_op jit(solution)/shard_map/all_to_all | solution.py:242
  514.3 22.3 %all-to-all-start.5 = ((bf16[64,16,256]{2,1,0:T(8,128)(2,1)}), bf16[64,16,256]{2,1,0:T(8,128)(2,1)S(1)}, u32[]{:S(2)}, u32[]{:S(2)}) async-start(bf16[64,16,256]{2,1,0:T(8,128)(2,1)} %bitcast.34), calls=%async_computation.5 | async-start | bytes 1048576 | tf_op jit(solution)/shard_map/all_to_all | solution.py:240
  536.6 23.6 %all-to-all-start.6 = ((bf16[64,16,256]{2,1,0:T(8,128)(2,1)}), bf16[64,16,256]{2,1,0:T(8,128)(2,1)S(1)}, u32[]{:S(2)}, u32[]{:S(2)}) async-start(bf16[64,16,256]{2,1,0:T(8,128)(2,1)} %bitcast.37), calls=%async_computation.6 | async-start | bytes 1048576 | tf_op jit(solution)/shard_map/all_to_all | solution.py:241
  560.2 6.1 copy-start.37
  560.2 6.1 copy-start.20
  560.2 222.3 %all-to-all-start.4 = ((bf16[64,16,2048]{2,1,0:T(8,128)(2,1)}), bf16[64,16,2048]{2,1,0:T(8,128)(2,1)}, u32[]{:S(2)}, u32[]{:S(2)}) async-start(bf16[64,16,2048]{2,1,0:T(8,128)(2,1)} %bitcast.620), calls=%async_computation.4 | async-start | bytes 8388608 | tf_op jit(solution)/shard_map/all_to_all | solution.py:239
  566.3 2.4 copy-start.14
  566.4 2.7 copy-start.33
  566.4 3.3 copy-start.30
  (16 other events, 20.5 us)
Sparse Core Ops, SparseCore 0:
  117.2 20.8 all-gather.7
  214.4 17.6 all-gather.5
where the time goes:
time: 809 us; the launch traced here: 798 us
  blocking collectives  208 us (26%)
  local copies, waits for them, and re-layouts  163 us (20%)
  matrix products  138 us (17%)
  waiting for transfers between devices  133 us (16%)
  other arithmetic  78.4 us (10%)
  starting transfers between devices  56.5 us (7%)
  between operations  15.3 us (2%)
    psum x1, blocking collectives, per_device(): total_params = lax.psum(local_params, ('dp', 'ctx'))  204 us
    all_to_all x1, waiting for transfers between devices, per_device(): lax.all_to_all(send_inputs, ('dp', 'ctx'), split_axis=0, concat_axis=0, t...  67 us
    dot_general x6, matrix products, block_step(): jnp.einsum('gjts,sgjp->tgjp', scores, head_vals, precision=PRECISE)  59.7 us
    scatter x8, local copies, waits for them, and re-layouts, spread_width(): jnp.zeros((slot_count, values.shape[1]), values.dtype).at[slots].set(values)  32.4 us
    dot_general x8, matrix products, block_step(): jnp.einsum('tgn,gjpn->tgjp', read_grp, state_four, precision=PRECISE)  30.6 us
    dot_general x6, matrix products, block_step(): jnp.einsum('sgjp,sgn->gjpn', weighted, write_grp, precision=PRECISE)  27.6 us
    another operation x50, other arithmetic  19 us
    dynamic_update_slice x14, local copies, waits for them, and re-layouts, run_blocks(): final_state, outputs = lax.scan(advance, first_state, pieces)  16.3 us
  transfers between devices with their start and end apart: 10, of which 8 were waited for; matrix products, arithmetic and copies ran while one was open for 13% of the time, Pallas kernels for 0%

commit v1 on v0

v1 whole, which is shorter than its diff:
```python
import math

import jax
import jax.numpy as jnp
from jax import lax
from jax.experimental import pallas as pl
from jax.experimental.pallas import tpu as pltpu
from jax.sharding import PartitionSpec as P

HEAD = 64
STATE = 256
BLOCK = 256
ROWS = 512
HEADS = 32
WIDTH = HEADS * HEAD
PEERS = 64
CAP = 16
SLOTS = PEERS * CAP
SMALL = 2 * STATE + 128
CHUNKS = 4
CHUNK = WIDTH // CHUNKS
MESH = pl.DeviceIdType.MESH
F32 = jnp.float32
BF16 = jnp.bfloat16
PRECISE = lax.Precision.HIGHEST


def nn(a, b, **kw):
    return lax.dot_general(a, b, (((1,), (0,)), ((), ())), preferred_element_type=F32, **kw)


def nt(a, b):
    return lax.dot_general(a, b, (((1,), (1,)), ((), ())), preferred_element_type=F32)


def tn(a, b):
    return lax.dot_general(a, b, (((0,), (0,)), ((), ())), preferred_element_type=F32)


def split(v):
    high = v.astype(BF16)
    return high, (v - high.astype(F32)).astype(BF16)


def both(product, a, b):
    if isinstance(a, tuple) and isinstance(b, tuple):
        return product(a[0], b[0]) + product(a[0], b[1]) + product(a[1], b[0])
    if isinstance(a, tuple):
        return product(a[0], b) + product(a[1], b)
    return product(a, b[0]) + product(a, b[1])


def iota(shape, dim):
    return lax.broadcasted_iota(jnp.int32, shape, dim)


def as_bf16(mask):
    return mask.astype(F32).astype(BF16)


def column(row):
    n = row.shape[1]
    return jnp.sum(jnp.where(iota((n, n), 0) == iota((n, n), 1), row, jnp.zeros((), row.dtype)), axis=1, keepdims=True)


def int_column(row):
    return column(row.astype(F32)).astype(jnp.int32)


def split_heads(ref, values, part=slice(None)):
    for h in range(HEADS):
        ref[h, :, part] = values[h : h + 1, :]


def join_heads(ref, part=slice(None)):
    return jnp.concatenate([ref[h, :, part] for h in range(HEADS)], axis=0)


def send_slot_row(place_row):
    target = lax.shift_right_logical(place_row, 9)
    ids = iota((PEERS, ROWS), 0)
    match = ids == target
    earlier = as_bf16(iota((ROWS, ROWS), 0) < iota((ROWS, ROWS), 1))
    before = nn(as_bf16(match), earlier)
    slot = jnp.sum(jnp.where(match, before + (ids * CAP).astype(F32), 0.0), axis=0, keepdims=True)
    return slot.astype(jnp.int32)


def send_slot_col(place_col):
    target = lax.shift_right_logical(place_col, 9)
    ids = iota((ROWS, PEERS), 1)
    match = ids == target
    earlier = as_bf16(iota((ROWS, ROWS), 1) < iota((ROWS, ROWS), 0))
    before = nn(earlier, as_bf16(match))
    slot = jnp.sum(jnp.where(match, before + (ids * CAP).astype(F32), 0.0), axis=1, keepdims=True)
    return slot.astype(jnp.int32)


def take_slot_row(anchor_col, anchor_row):
    source_row = lax.shift_right_logical(anchor_row, 9)
    same = lax.shift_right_logical(anchor_col, 9) == source_row
    before = jnp.where(same & (anchor_col < anchor_row), 1.0, 0.0)
    return source_row * CAP + jnp.sum(before, axis=0, keepdims=True).astype(jnp.int32)


def take_slot_col(anchor_col, anchor_row):
    source_col = lax.shift_right_logical(anchor_col, 9)
    same = source_col == lax.shift_right_logical(anchor_row, 9)
    before = jnp.where(same & (anchor_row < anchor_col), 1.0, 0.0)
    return source_col * CAP + jnp.sum(before, axis=1, keepdims=True).astype(jnp.int32)


def softplus(v):
    return jnp.maximum(v, 0.0) + jnp.log1p(jnp.exp(-jnp.abs(v)))


def starts_between(len_ref, low, high):
    first = len_ref[0, 0]
    second = first + len_ref[0, 1]
    count = jnp.zeros(jnp.broadcast_shapes(jnp.shape(low), jnp.shape(high)), F32)
    for bound in (0, first, second):
        count = count + jnp.where((bound >= low) & (bound <= high), 1.0, 0.0)
    return count


def running_sum(rate):
    upto = (iota((BLOCK, BLOCK), 0) <= iota((BLOCK, BLOCK), 1)).astype(F32)
    return nn(rate, upto, precision=PRECISE)


def peer_copies(me, source, target, send_sem, recv_sem):
    @pl.loop(1, PEERS)
    def _(k):
        peer = lax.rem(me + k, PEERS)
        pltpu.make_async_remote_copy(
            src_ref=source.at[pl.ds(pl.multiple_of(peer * CAP, CAP), CAP)],
            dst_ref=target.at[pl.ds(pl.multiple_of(me * CAP, CAP), CAP)],
            send_sem=send_sem,
            recv_sem=recv_sem,
            device_id={"dp": peer // 2, "ctx": lax.rem(peer, 2)},
            device_id_type=MESH,
        ).start()

    own = pl.ds(pl.multiple_of(me * CAP, CAP), CAP)
    target[own, :] = source[own, :]


def wait_peers(ref, sem):
    view = ref.at[pl.ds(0, SLOTS - CAP)]
    pltpu.make_async_copy(view, view, sem).wait()


def layer_kernel(
    len_ref, place_ref, anchor_ref,
    x_ref, w_ref, r_ref, s_ref, cot_ref, dec_ref, bias_ref, skip_ref,
    y_ref, gx_ref, gw_ref, gr_ref, gs_ref, par_ref,
    snd_s, snd_x, lnd_s, lnd_x, bck_s, bck_x, ret_s, ret_x, edge_out, edge_in,
    perm_ref, pick_ref, xt_ref, bc_ref, u_ref, scale_ref, gain_ref,
    run_ref, wide_ref, step_ref, ent_ref, lev_ref, keep_ref, mask_ref, gram_ref, dgram_ref,
    dw_ref, dr_ref, dx_ref, yy_ref, xi_ref, xs_ref, kd_ref, gg_ref, dbc_ref,
    send_sem, recv_sem, back_send_sem, back_recv_sem, edge_send_sem, edge_recv_sem,
):
    dp, ctx = lax.axis_index("dp"), lax.axis_index("ctx")
    me = dp * 2 + ctx
    barrier = pltpu.get_barrier_semaphore()

    @pl.loop(1, PEERS)
    def _(k):
        peer = lax.rem(me + k, PEERS)
        pl.semaphore_signal(
            barrier, inc=1, device_id={"dp": peer // 2, "ctx": lax.rem(peer, 2)}, device_id_type=MESH
        )

    perm_ref[...] = as_bf16(iota((SLOTS, ROWS), 0) == send_slot_row(place_ref[...]))
    snd_s[:, :STATE] = nn(perm_ref[...], w_ref[...]).astype(BF16)
    snd_s[:, STATE : 2 * STATE] = nn(perm_ref[...], r_ref[...]).astype(BF16)
    steps = jnp.concatenate([s_ref[...], jnp.zeros((128 - HEADS, ROWS), BF16)], axis=0)
    snd_s[:, 2 * STATE :] = nt(perm_ref[...], steps).astype(BF16)
    pl.semaphore_wait(barrier, PEERS - 1)
    peer_copies(me, snd_s, lnd_s, send_sem.at[CHUNKS], recv_sem.at[CHUNKS])
    for k in range(CHUNKS):
        for half in range(CHUNK // 256):
            inside = slice(half * 256, half * 256 + 256)
            cols = slice(k * CHUNK + half * 256, k * CHUNK + half * 256 + 256)
            snd_x[k, :, inside] = nn(perm_ref[...], x_ref[:, cols]).astype(BF16)
        peer_copies(me, snd_x.at[k], lnd_x.at[k], send_sem.at[k], recv_sem.at[k])

    base = ctx * ROWS
    is_late = (ctx == 1).astype(F32)
    is_early = (ctx == 0).astype(F32)
    parts = (slice(0, BLOCK), slice(BLOCK, 2 * BLOCK))
    anchor_row, anchor_col = anchor_ref[...], int_column(anchor_ref[...])
    take_r = take_slot_row(anchor_col, anchor_row)
    pick_ref[...] = as_bf16(iota((SLOTS, ROWS), 0) == take_r)
    take_c = take_slot_col(anchor_col, anchor_row)
    pick = as_bf16(iota((ROWS, SLOTS), 1) == take_c)

    wait_peers(lnd_s, recv_sem.at[CHUNKS])
    bc_ref[...] = nn(pick, lnd_s[:, : 2 * STATE]).astype(BF16)
    u_ref[...] = tn(lnd_s[:, 2 * STATE :], pick_ref[...])[:HEADS] + column(bias_ref[...])
    u = u_ref[...]
    step = softplus(u)
    decay = -jnp.exp(column(dec_ref[...]))
    split_heads(gain_ref, jnp.broadcast_to(column(skip_ref[...]), (HEADS, BLOCK)))
    rate = decay * step
    split_heads(step_ref, step)
    keeps, runs = [], []
    for c in range(2):
        part = parts[c]
        first = base + c * BLOCK
        last = first + BLOCK - 1
        run = running_sum(rate[:, part])
        runs.append(run)
        split_heads(run_ref, run, part)
        pos = first + iota((1, BLOCK), 1)
        pos_col = first + iota((BLOCK, 1), 0)
        open_start = (starts_between(len_ref, jnp.full((1, BLOCK), first, jnp.int32), pos) == 0).astype(F32)
        open_end = (starts_between(len_ref, pos + 1, jnp.full((1, BLOCK), last, jnp.int32)) == 0).astype(F32)
        run_end = run[:, BLOCK - 1 :]
        split_heads(ent_ref, jnp.exp(run) * open_start, part)
        split_heads(lev_ref, jnp.exp(run_end - run) * step[:, part] * open_end, part)
        kept = jnp.exp(run_end) * open_start[:, BLOCK - 1 :]
        keeps.append(kept)
        split_heads(keep_ref, jnp.broadcast_to(kept, (HEADS, BLOCK)), part)
        crossing = starts_between(len_ref, pos + 1, pos_col)
        mask_ref[c] = jnp.where((pos_col >= pos) & (crossing == 0), 0.0, -1e30)
        tall = jnp.concatenate([run, jnp.zeros((128 - HEADS, BLOCK), F32)], axis=0).T
        for h in range(HEADS):
            wide_ref[h, part, :] = jnp.broadcast_to(tall[:, h : h + 1], (BLOCK, 128))
        gram_ref[c] = nt(bc_ref[part, STATE:], bc_ref[part, :STATE])
        dgram_ref[c] = jnp.zeros((BLOCK, BLOCK), F32)
        dw_ref[part, :] = jnp.zeros((BLOCK, STATE), F32)
        dr_ref[part, :] = jnp.zeros((BLOCK, STATE), F32)

    whole = jnp.concatenate([runs[0], runs[1] + runs[0][:, BLOCK - 1 :]], axis=1)
    pos = base + iota((1, ROWS), 1)
    open_end = (starts_between(len_ref, pos + 1, jnp.full((1, ROWS), base + ROWS - 1, jnp.int32)) == 0).astype(F32)
    open_start = (starts_between(len_ref, jnp.full((1, ROWS), base, jnp.int32), pos) == 0).astype(F32)
    leave_all = jnp.exp(whole[:, ROWS - 1 :] - whole) * step * open_end
    enter_all = jnp.exp(whole) * open_start
    split_heads(scale_ref, is_early * leave_all + is_late * enter_all)

    def scaled(h, values):
        four = [values[HEAD * i : HEAD * i + HEAD] * scale_ref[h + i] for i in range(4)]
        return split(jnp.concatenate(four, axis=0))

    def edge_copy(k):
        return pltpu.make_async_remote_copy(
            src_ref=edge_out.at[k],
            dst_ref=edge_in.at[k],
            send_sem=edge_send_sem.at[k],
            recv_sem=edge_recv_sem.at[k],
            device_id={"dp": dp, "ctx": 1 - ctx},
            device_id_type=MESH,
        )

    def open_chunk(k):
        wait_peers(lnd_x.at[k], recv_sem.at[k])
        for q in range(CHUNK // 256):
            inside = slice(q * 256, q * 256 + 256)
            rows = slice(k * CHUNK + q * 256, k * CHUNK + q * 256 + 256)
            xt_ref[rows, :] = tn(lnd_x[k, :, inside], pick_ref[...]).astype(BF16)
        head = k * CHUNK // HEAD

        @pl.when(ctx == 0)
        def _():
            for q in range(CHUNK // 256):
                rows = slice(k * CHUNK + q * 256, k * CHUNK + q * 256 + 256)
                values = scaled(head + 4 * q, xt_ref[rows, :].astype(F32))
                edge_out[k, q * 256 : q * 256 + 256, :] = both(nn, values, bc_ref[:, :STATE])

        @pl.when(ctx == 1)
        def _():
            for q in range(CHUNK // 256):
                rows = slice(k * CHUNK + q * 256, k * CHUNK + q * 256 + 256)
                values = scaled(head + 4 * q, cot_ref[:, rows].astype(F32).T)
                edge_out[k, q * 256 : q * 256 + 256, :] = both(nn, values, bc_ref[:, STATE:])

        edge_copy(k).start()

    def rows_of(ref, j, part):
        return jnp.concatenate(
            [jnp.broadcast_to(ref[2 * j + i, :, part], (HEAD, BLOCK)) for i in range(2)], axis=0
        )

    def pair(k, near):
        j = k * (CHUNK // 128) + near
        rows = pl.ds(pl.multiple_of(j * 128, 128), 128)
        edge = edge_in[k, pl.ds(pl.multiple_of(near * 128, 128), 128), :]
        x_t = [xt_ref[rows, part] for part in parts]
        x_f = [v.astype(F32) for v in x_t]
        d_n = [cot_ref[part, rows] for part in parts]
        d_f = [v.astype(F32).T for v in d_n]
        d_t = [v.astype(BF16) for v in d_f]
        gain = rows_of(gain_ref, j, slice(None))
        ent = [rows_of(ent_ref, j, part) for part in parts]
        lev = [rows_of(lev_ref, j, part) for part in parts]
        keep = [rows_of(keep_ref, j, part) for part in parts]
        w_t = [split(x_f[c] * lev[c]) for c in range(2)]
        v_t = [split(d_f[c] * ent[c]) for c in range(2)]
        state0 = edge * is_late
        state1 = both(nn, w_t[0], bc_ref[parts[0], :STATE]) + keep[0] * state0
        grad1 = edge * is_early
        grad0 = both(nn, v_t[1], bc_ref[parts[1], STATE:]) + keep[1] * grad1
        states, grads = (state0, state1), (grad0, grad1)
        upper = iota((128, BLOCK), 0) < HEAD
        for c in range(2):
            part = parts[c]
            y_parts, dx_parts = [], []
            for i in range(2):
                own = slice(HEAD * i, HEAD * i + HEAD)
                tall = wide_ref[2 * j + i, part, :]
                gap = jnp.concatenate([tall, tall], axis=1) - run_ref[2 * j + i, :, part]
                decayed = jnp.exp(gap + mask_ref[c]) * step_ref[2 * j + i, :, part]
                scores = split(gram_ref[c] * decayed)
                y_parts.append(both(nt, x_t[c][own], scores))
                dx_parts.append(both(nn, d_t[c][own], scores))
                only = jnp.where(upper if i == 0 else jnp.logical_not(upper), x_f[c], 0.0).astype(BF16)
                dgram_ref[c] += nn(d_n[c], only) * decayed
            state_b, grad_b = split(states[c]), split(grads[c])
            y_f = jnp.concatenate(y_parts, axis=0) + both(nt, state_b, bc_ref[part, STATE:]) * ent[c]
            dx_i = jnp.concatenate(dx_parts, axis=0)
            dx_s = both(nt, grad_b, bc_ref[part, :STATE]) * lev[c]
            yy, xi, xs, gg = d_f[c] * y_f, x_f[c] * dx_i, x_f[c] * dx_s, x_f[c] * d_f[c]
            kd = states[c] * grads[c]
            for i in range(2):
                own = slice(HEAD * i, HEAD * i + HEAD)
                one = 2 * j + i
                yy_ref[one, :, part] = jnp.sum(yy[own], axis=0, keepdims=True)
                xi_ref[one, :, part] = jnp.sum(xi[own], axis=0, keepdims=True)
                xs_ref[one, :, part] = jnp.sum(xs[own], axis=0, keepdims=True)
                gg_ref[one, :, part] = jnp.sum(gg[own], axis=0, keepdims=True)
                kd_ref[one, :, part] = jnp.sum(kd[own], axis=0, keepdims=True)
            y_ref[part, rows] = (y_f + gain * x_f[c]).T.astype(BF16)
            dx_ref[rows, part] = (dx_i + dx_s + gain * d_f[c]).astype(BF16)
            dw_ref[part, :] += both(tn, w_t[c], grad_b)
            dr_ref[part, :] += both(tn, v_t[c], state_b)

    def scan_chunk(k):
        edge_copy(k).wait()

        @pl.loop(0, CHUNK // 128)
        def _(near):
            pair(k, near)

        for q in range(CHUNK // 256):
            inside = slice(q * 256, q * 256 + 256)
            rows = slice(k * CHUNK + q * 256, k * CHUNK + q * 256 + 256)
            bck_x[k, :, inside] = nt(pick_ref[...], dx_ref[rows, :]).astype(BF16)
        peer_copies(me, bck_x.at[k], ret_x.at[k], back_send_sem.at[k], back_recv_sem.at[k])

    for k in range(CHUNKS):
        open_chunk(k)
        if k:
            scan_chunk(k - 1)
    scan_chunk(CHUNKS - 1)

    later = (iota((BLOCK, BLOCK), 0) >= iota((BLOCK, BLOCK), 1)).astype(F32)
    sooner = (iota((BLOCK, BLOCK), 0) < iota((BLOCK, BLOCK), 1)).astype(F32)
    drates = []
    yy, xi, xs = join_heads(yy_ref), join_heads(xi_ref), join_heads(xs_ref)
    for c in range(2):
        part = slice(c * BLOCK, c * BLOCK + BLOCK)
        dg = split(dgram_ref[c])
        write, read = bc_ref[part, :STATE], bc_ref[part, STATE:]
        dbc_ref[part, :STATE] = (dw_ref[part, :] + both(tn, dg, read)).astype(BF16)
        dbc_ref[part, STATE:] = (dr_ref[part, :] + both(nn, dg, write)).astype(BF16)
        through = keeps[c] * jnp.sum(join_heads(kd_ref, part), axis=1, keepdims=True)
        drate = (
            nn(yy[:, part] - xi[:, part], later, precision=PRECISE)
            + nn(xs[:, part], sooner, precision=PRECISE)
            + through
        )
        pos = base + c * BLOCK + iota((1, BLOCK), 1)
        drates.append(drate * (starts_between(len_ref, pos, pos) == 0).astype(F32))
    drate = jnp.concatenate(drates, axis=1)
    dstep = decay * drate + (xi + xs) / step
    du = dstep / (1.0 + jnp.exp(-u))
    lane, head = iota((HEADS, 128), 1), iota((HEADS, 128), 0)
    partial = (
        jnp.where(lane == HEADS + head, jnp.sum(drate * rate, axis=1, keepdims=True), 0.0)
        + jnp.where(lane == 2 * HEADS + head, jnp.sum(du, axis=1, keepdims=True), 0.0)
        + jnp.where(lane == 3 * HEADS + head, jnp.sum(join_heads(gg_ref), axis=1, keepdims=True), 0.0)
    )
    partial = jnp.sum(partial, axis=0, keepdims=True)
    high = partial.astype(BF16).astype(F32)
    middle = (partial - high).astype(BF16).astype(F32)
    low = partial - high - middle
    place = iota((SLOTS, 128), 0) % CAP
    extra = jnp.where(place == 0, high, jnp.where(place == 1, middle, jnp.where(place == 2, low, 0.0)))
    bck_s[:, : 2 * STATE] = nn(pick_ref[...], dbc_ref[...]).astype(BF16)
    du_wide = jnp.concatenate([du, jnp.zeros((128 - HEADS, ROWS), F32)], axis=0).astype(BF16)
    bck_s[:, 2 * STATE :] = (nt(pick_ref[...], du_wide) + extra).astype(BF16)
    peer_copies(me, bck_s, ret_s, back_send_sem.at[CHUNKS], back_recv_sem.at[CHUNKS])

    perm = as_bf16(iota((ROWS, SLOTS), 1) == send_slot_col(int_column(place_ref[...])))
    for k in range(CHUNKS):
        wait_peers(ret_x.at[k], back_recv_sem.at[k])
        for q in range(CHUNK // 256):
            inside = slice(q * 256, q * 256 + 256)
            cols = slice(k * CHUNK + q * 256, k * CHUNK + q * 256 + 256)
            gx_ref[:, cols] = nn(perm, ret_x[k, :, inside]).astype(BF16)
    wait_peers(ret_s, back_recv_sem.at[CHUNKS])
    gw_ref[...] = nn(perm, ret_s[:, :STATE]).astype(BF16)
    gr_ref[...] = nn(perm, ret_s[:, STATE : 2 * STATE]).astype(BF16)
    gs_ref[...] = tn(ret_s[:, 2 * STATE :], perm_ref[...])[:HEADS].astype(BF16)
    total = jnp.sum(ret_s[:, 2 * STATE :].astype(F32), axis=0, keepdims=True)
    par_ref[...] = total * (1.0 / math.sqrt(ROWS * PEERS * HEAD))
    for k in range(CHUNKS):
        wait_peers(snd_x.at[k], send_sem.at[k])
        wait_peers(bck_x.at[k], back_send_sem.at[k])
    wait_peers(snd_s, send_sem.at[CHUNKS])
    wait_peers(bck_s, back_send_sem.at[CHUNKS])


def sds(shape, dtype):
    return jax.ShapeDtypeStruct(shape, dtype)


def vmem(n):
    return [pl.BlockSpec(memory_space=pltpu.VMEM)] * n


def per_device(
    head_inputs, write_vecs, read_vecs, step_raw, decay_log, step_bias, skip_gain,
    out_cotangent, rollout_lengths, plan_place, plan_anchor,
):
    small, large = (SLOTS, SMALL), (CHUNKS, SLOTS, CHUNK)
    per_head = pltpu.VMEM((HEADS, 1, ROWS), F32)
    square = pltpu.VMEM((2, BLOCK, BLOCK), F32)
    transfers = [pltpu.VMEM(shape, BF16) for _ in range(4) for shape in (small, large)]
    edges = [pltpu.VMEM((CHUNKS, CHUNK, STATE), F32)] * 2
    layer_out, grad_x, grad_w, grad_r, grad_s, params = pl.pallas_call(
        layer_kernel,
        out_shape=(
            sds((ROWS, WIDTH), BF16),
            sds((ROWS, WIDTH), BF16),
            sds((ROWS, STATE), BF16),
            sds((ROWS, STATE), BF16),
            sds((HEADS, ROWS), BF16),
            sds((1, 128), F32),
        ),
        in_specs=[pl.BlockSpec(memory_space=pltpu.SMEM)] + vmem(10),
        out_specs=tuple(vmem(6)),
        scratch_shapes=[
            *transfers,
            *edges,
            pltpu.VMEM((SLOTS, ROWS), BF16),
            pltpu.VMEM((SLOTS, ROWS), BF16),
            pltpu.VMEM((WIDTH, ROWS), BF16),
            pltpu.VMEM((ROWS, 2 * STATE), BF16),
            pltpu.VMEM((HEADS, ROWS), F32),
            per_head,
            pltpu.VMEM((HEADS, 1, BLOCK), F32),
            per_head,
            pltpu.VMEM((HEADS, ROWS, 128), F32),
            per_head,
            per_head,
            per_head,
            per_head,
            square,
            square,
            square,
            pltpu.VMEM((ROWS, STATE), F32),
            pltpu.VMEM((ROWS, STATE), F32),
            pltpu.VMEM((WIDTH, ROWS), BF16),
            per_head,
            per_head,
            per_head,
            per_head,
            per_head,
            pltpu.VMEM((ROWS, 2 * STATE), BF16),
            pltpu.SemaphoreType.DMA((CHUNKS + 1,)),
            pltpu.SemaphoreType.DMA((CHUNKS + 1,)),
            pltpu.SemaphoreType.DMA((CHUNKS + 1,)),
            pltpu.SemaphoreType.DMA((CHUNKS + 1,)),
            pltpu.SemaphoreType.DMA((CHUNKS,)),
            pltpu.SemaphoreType.DMA((CHUNKS,)),
        ],
        compiler_params=pltpu.CompilerParams(
            collective_id=0, has_side_effects=True, vmem_limit_bytes=60 * 1024 * 1024
        ),
        name="layer",
    )(
        rollout_lengths, plan_place.reshape(1, ROWS), plan_anchor.reshape(1, ROWS),
        head_inputs, write_vecs, read_vecs, step_raw.T, out_cotangent,
        decay_log.reshape(1, HEADS), step_bias.reshape(1, HEADS), skip_gain.reshape(1, HEADS),
    )
    return (layer_out, grad_x, grad_w, grad_r, grad_s.T, params[0, HEADS:].reshape(3, HEADS))


def solution(mesh):
    rows = P(("dp", "ctx"), "tp")
    return jax.shard_map(
        per_device,
        mesh=mesh,
        in_specs=(
            rows, rows, rows, rows, P("tp"), P("tp"), P("tp"), rows, P("dp", None), P(("dp", "ctx")), P(("dp", "ctx")),
        ),
        out_specs=(rows, rows, rows, rows, rows, P(None, "tp")),
        check_vma=False,
    )
```

time: 809 us -> 265 us (0.33); the launches traced: 798 us -> 262 us
  Pallas kernels: 0 us -> 254 us
  blocking collectives: 208 us -> 0 us
  local copies, waits for them, and re-layouts: 163 us -> 8.02 us
  matrix products: 138 us -> 0 us
  waiting for transfers between devices: 133 us -> 0 us
  other arithmetic: 78.4 us -> 0 us
  starting transfers between devices: 56.5 us -> 0 us
  between operations: 15.3 us -> 0.66 us
    pallas_call x0 -> x1, Pallas kernels: none -> 254 us  [per_device(): pl.pallas_call(layer_kernel, out_shape=(sds((ROWS, WIDTH), BF16), sds((RO...]
    psum x1 -> x0, blocking collectives: 204 us -> none  [per_device(): total_params = lax.psum(local_params, ('dp', 'ctx'))]
    dot_general x31 -> x0, matrix products: 138 us -> none  [the longest x6 59.7 us: block_step(): jnp.einsum('gjts,sgjp->tgjp', scores, head_vals, precision=PRECISE)]
    all_to_all x8 -> x0, waiting for transfers between devices: 129 us -> none  [the longest x1 67 us: per_device(): lax.all_to_all(send_inputs, ('dp', 'ctx'), split_axis=0, concat_axis=0, t...]
    all_to_all x8 -> x0, starting transfers between devices: 56.2 us -> none  [the longest x1 13 us: per_device(): lax.all_to_all(send_steps, ('dp', 'ctx'), split_axis=0, concat_axis=0, ti...]
    scatter x8 -> x0, local copies, waits for them, and re-layouts: 32.4 us -> none  [spread_width(): jnp.zeros((slot_count, values.shape[1]), values.dtype).at[slots].set(values)]
    gather x8 -> x0, local copies, waits for them, and re-layouts: 28 us -> none  [the longest x1 7.95 us: per_device(): returning[0][send_slot]]
    mul x29 -> x0, other arithmetic: 25.3 us -> none  [the longest x4 6.28 us: block_step(): (leaving * step_size).reshape(row_count, group_count, per_group, 1)]
  transfers between devices with their start and end apart: 10 -> 0, of which waited for: 8 -> 0; matrix products, arithmetic and copies ran while one was open for 13% -> 0% of each run, Pallas kernels for 0% -> 0%
where the time goes in v1:
time: 265 us; the launch traced here: 262 us
  Pallas kernels  254 us (96%)
  local copies, waits for them, and re-layouts  8.02 us (3%)
    pallas_call x1, Pallas kernels, per_device(): pl.pallas_call(layer_kernel, out_shape=(sds((ROWS, WIDTH), BF16), sds((RO...  254 us
    unnamed x13, local copies, waits for them, and re-layouts  6.66 us

profile of v1, /device:TPU:1, one launch (start us, length us, event | category | flops | bytes accessed | tf_op | source)
XLA Modules:
  0.0 262.4 jit_solution(10725679511638883966)
XLA Ops:
  0.6 253.7 %layer.1 = (bf16[512,2048]{1,0:T(8,128)(2,1)}, bf16[512,2048]{1,0:T(8,128)(2,1)}, bf16[512,256]{1,0:T(8,128)(2,1)}, bf16[512,256]{1,0:T(8,128)(2,1)}, bf16[32,512]{1,0:T(8,128)(2,1)}, /*index=5*/f32[1,128]{1,0:T(1,128)}) custom-call(s32[1,3]{1,0:T(1,128)} %len_ref.1, s32[1,512]{1,0:T(1,128)} %bitcast.9, s32[1,512]{1,0:T(1,128)} %bitcast.10, ...), custom_call_target="tpu_custom_call" | custom-call | tf_op jit(solution)/shard_map/layer/pallas_call | solution.py:433
  254.3 0.7 slice_reduce_fusion
  255.0 0.7 reshape_squeeze.3
  255.7 0.0 copy-start
  255.7 3.3 %copy.22 = bf16[512,2048]{1,0:T(8,128)(2,1)} copy(bf16[512,2048]{1,0:T(8,128)(2,1)} %get-tuple-element.24) | data formatting | bytes 4194304
  259.0 0.0 copy-done
  259.0 0.0 copy-start.2
  259.0 0.0 copy-start.1
  259.0 0.0 copy-start.3
  259.0 1.3 copy.23
  260.3 0.0 copy-done.2
  260.3 0.7 copy.24
  261.0 0.0 copy-done.1
  261.0 0.7 copy.25
  261.8 0.0 copy-done.3
  261.8 0.6 copy.26
Async XLA Ops:
  255.7 3.3 %copy-start = (bf16[512,2048]{1,0:T(8,128)(2,1)S(1)}, bf16[512,2048]{1,0:T(8,128)(2,1)}, u32[]{:S(2)}) copy-start(bf16[512,2048]{1,0:T(8,128)(2,1)} %get-tuple-element.25) | copy-start | bytes 6291460
  259.0 1.3 copy-start.2
  259.0 2.0 copy-start.1
  259.0 2.7 %copy-start.3 = (bf16[32,512]{1,0:T(8,128)(2,1)S(1)}, bf16[32,512]{1,0:T(8,128)(2,1)}, u32[]{:S(2)}) copy-start(bf16[32,512]{1,0:T(8,128)(2,1)} %get-tuple-element.16) | copy-start | bytes 98308

commit v2 on v1

--- a/solution.py
+++ b/solution.py
@@ -16,7 +16,8 @@
 PEERS = 64
 CAP = 16
 SLOTS = PEERS * CAP
-SMALL = 2 * STATE + 128
+SMALL = 2 * STATE
+QUART = CAP // 4
 CHUNKS = 4
 CHUNK = WIDTH // CHUNKS
 MESH = pl.DeviceIdType.MESH
@@ -145,6 +146,56 @@
     target[own, :] = source[own, :]
 
 
+def block_copies(me, source, target, send_sem, recv_sem):
+    single = source.shape[0] == 1
+
+    @pl.loop(1, PEERS)
+    def _(k):
+        peer = lax.rem(me + k, PEERS)
+        pltpu.make_async_remote_copy(
+            src_ref=source.at[0 if single else peer],
+            dst_ref=target.at[me],
+            send_sem=send_sem,
+            recv_sem=recv_sem,
+            device_id={"dp": peer // 2, "ctx": lax.rem(peer, 2)},
+            device_id_type=MESH,
+        ).start()
+
+    target[me] = source[0 if single else me]
+
+
+def wait_blocks(ref, sem):
+    view = ref.at[pl.ds(0, PEERS - 1)]
+    pltpu.make_async_copy(view, view, sem).wait()
+
+
+def quarter_picks(slot):
+    at = iota((PEERS * QUART, ROWS), 0)
+    first = (at % PEERS) * CAP + (at // PEERS) * 4
+    return [as_bf16(slot == first + j) for j in range(4)]
+
+
+def pack_steps(steps, picks, stage, out):
+    total = None
+    for j in range(4):
+        pieces = [steps if i == j else jnp.zeros((HEADS, ROWS), BF16) for i in range(4)]
+        term = nt(picks[j], jnp.concatenate(pieces, axis=0))
+        total = term if total is None else total + term
+    for i in range(QUART):
+        stage[:, i, :] = total[PEERS * i : PEERS * i + PEERS]
+    out[...] = stage[...].astype(BF16)
+
+
+def unpack_steps(arrived, picks, stage):
+    stage[...] = arrived[...].astype(F32)
+    rows = jnp.concatenate([stage[:, i, :] for i in range(QUART)], axis=0).astype(BF16)
+    total = None
+    for j in range(4):
+        term = tn(rows, picks[j])[HEADS * j : HEADS * j + HEADS]
+        total = term if total is None else total + term
+    return total
+
+
 def wait_peers(ref, sem):
     view = ref.at[pl.ds(0, SLOTS - CAP)]
     pltpu.make_async_copy(view, view, sem).wait()
@@ -154,6 +205,7 @@
     len_ref, place_ref, anchor_ref,
     x_ref, w_ref, r_ref, s_ref, cot_ref, dec_ref, bias_ref, skip_ref,
     y_ref, gx_ref, gw_ref, gr_ref, gs_ref, par_ref,
+    snd_t, lnd_t, bck_t, ret_t, par_out, par_in, stage,
     snd_s, snd_x, lnd_s, lnd_x, bck_s, bck_x, ret_s, ret_x, edge_out, edge_in,
     perm_ref, pick_ref, xt_ref, bc_ref, u_ref, scale_ref, gain_ref,
     run_ref, wide_ref, step_ref, ent_ref, lev_ref, keep_ref, mask_ref, gram_ref, dgram_ref,
@@ -171,12 +223,14 @@
             barrier, inc=1, device_id={"dp": peer // 2, "ctx": lax.rem(peer, 2)}, device_id_type=MESH
         )
 
-    perm_ref[...] = as_bf16(iota((SLOTS, ROWS), 0) == send_slot_row(place_ref[...]))
+    send_r = send_slot_row(place_ref[...])
+    perm_ref[...] = as_bf16(iota((SLOTS, ROWS), 0) == send_r)
+    send_picks = quarter_picks(send_r)
+    pack_steps(s_ref[...], send_picks, stage, snd_t)
     snd_s[:, :STATE] = nn(perm_ref[...], w_ref[...]).astype(BF16)
     snd_s[:, STATE : 2 * STATE] = nn(perm_ref[...], r_ref[...]).astype(BF16)
-    steps = jnp.concatenate([s_ref[...], jnp.zeros((128 - HEADS, ROWS), BF16)], axis=0)
-    snd_s[:, 2 * STATE :] = nt(perm_ref[...], steps).astype(BF16)
     pl.semaphore_wait(barrier, PEERS - 1)
+    block_copies(me, snd_t, lnd_t, send_sem.at[CHUNKS + 1], recv_sem.at[CHUNKS + 1])
     peer_copies(me, snd_s, lnd_s, send_sem.at[CHUNKS], recv_sem.at[CHUNKS])
     for k in range(CHUNKS):
         for half in range(CHUNK // 256):
@@ -196,8 +250,10 @@
     pick = as_bf16(iota((ROWS, SLOTS), 1) == take_c)
 
     wait_peers(lnd_s, recv_sem.at[CHUNKS])
-    bc_ref[...] = nn(pick, lnd_s[:, : 2 * STATE]).astype(BF16)
-    u_ref[...] = tn(lnd_s[:, 2 * STATE :], pick_ref[...])[:HEADS] + column(bias_ref[...])
+    wait_blocks(lnd_t, recv_sem.at[CHUNKS + 1])
+    bc_ref[...] = nn(pick, lnd_s[...]).astype(BF16)
+    take_picks = quarter_picks(take_r)
+    u_ref[...] = unpack_steps(lnd_t, take_picks, stage) + column(bias_ref[...])
     u = u_ref[...]
     step = softplus(u)
     decay = -jnp.exp(column(dec_ref[...]))
@@ -382,16 +438,12 @@
         + jnp.where(lane == 2 * HEADS + head, jnp.sum(du, axis=1, keepdims=True), 0.0)
         + jnp.where(lane == 3 * HEADS + head, jnp.sum(join_heads(gg_ref), axis=1, keepdims=True), 0.0)
     )
-    partial = jnp.sum(partial, axis=0, keepdims=True)
-    high = partial.astype(BF16).astype(F32)
-    middle = (partial - high).astype(BF16).astype(F32)
-    low = partial - high - middle
-    place = iota((SLOTS, 128), 0) % CAP
-    extra = jnp.where(place == 0, high, jnp.where(place == 1, middle, jnp.where(place == 2, low, 0.0)))
-    bck_s[:, : 2 * STATE] = nn(pick_ref[...], dbc_ref[...]).astype(BF16)
-    du_wide = jnp.concatenate([du, jnp.zeros((128 - HEADS, ROWS), F32)], axis=0).astype(BF16)
-    bck_s[:, 2 * STATE :] = (nt(pick_ref[...], du_wide) + extra).astype(BF16)
+    par_out[0] = jnp.sum(partial, axis=0, keepdims=True)
+    block_copies(me, par_out, par_in, back_send_sem.at[CHUNKS + 2], back_recv_sem.at[CHUNKS + 2])
+    bck_s[...] = nn(pick_ref[...], dbc_ref[...]).astype(BF16)
     peer_copies(me, bck_s, ret_s, back_send_sem.at[CHUNKS], back_recv_sem.at[CHUNKS])
+    pack_steps(du.astype(BF16), quarter_picks(take_slot_row(int_column(anchor_ref[...]), anchor_ref[...])), stage, bck_t)
+    block_copies(me, bck_t, ret_t, back_send_sem.at[CHUNKS + 1], back_recv_sem.at[CHUNKS + 1])
 
     perm = as_bf16(iota((ROWS, SLOTS), 1) == send_slot_col(int_column(place_ref[...])))
     for k in range(CHUNKS):
@@ -402,15 +454,47 @@
             gx_ref[:, cols] = nn(perm, ret_x[k, :, inside]).astype(BF16)
     wait_peers(ret_s, back_recv_sem.at[CHUNKS])
     gw_ref[...] = nn(perm, ret_s[:, :STATE]).astype(BF16)
-    gr_ref[...] = nn(perm, ret_s[:, STATE : 2 * STATE]).astype(BF16)
-    gs_ref[...] = tn(ret_s[:, 2 * STATE :], perm_ref[...])[:HEADS].astype(BF16)
-    total = jnp.sum(ret_s[:, 2 * STATE :].astype(F32), axis=0, keepdims=True)
-    par_ref[...] = total * (1.0 / math.sqrt(ROWS * PEERS * HEAD))
+    gr_ref[...] = nn(perm, ret_s[:, STATE:]).astype(BF16)
+    wait_blocks(par_in, back_recv_sem.at[CHUNKS + 2])
+    total = jnp.sum(par_in[...], axis=0) * (1.0 / math.sqrt(ROWS * PEERS * HEAD))
+    for k in range(3):
+        par_ref[k : k + 1, :] = total[:, HEADS * (k + 1) : HEADS * (k + 2)]
+    wait_blocks(ret_t, back_recv_sem.at[CHUNKS + 1])
+    gs_ref[...] = unpack_steps(ret_t, quarter_picks(send_slot_row(place_ref[...])), stage).astype(BF16)
     for k in range(CHUNKS):
         wait_peers(snd_x.at[k], send_sem.at[k])
         wait_peers(bck_x.at[k], back_send_sem.at[k])
     wait_peers(snd_s, send_sem.at[CHUNKS])
     wait_peers(bck_s, back_send_sem.at[CHUNKS])
+    wait_blocks(snd_t, send_sem.at[CHUNKS + 1])
+    wait_blocks(bck_t, back_send_sem.at[CHUNKS + 1])
+    wait_blocks(par_in, back_send_sem.at[CHUNKS + 2])
+
+
+def finish_kernel(*refs):
+    count = (len(refs) - 2) // 3
+    groups = [refs[count * g : count * g + count] for g in range(3)]
+    into_sem, out_sem = refs[-2:]
+    pieces = []
+    for source, target, middle in zip(*groups):
+        parts = 4 if source.shape == (ROWS, WIDTH) else 1
+        rows = source.shape[0] // parts
+        for p in range(parts):
+            part = pl.ds(p * rows, rows)
+            n = len(pieces)
+            pieces.append(
+                (
+                    pltpu.make_async_copy(source.at[part], middle.at[part], into_sem.at[n]),
+                    pltpu.make_async_copy(middle.at[part], target.at[part], out_sem.at[n]),
+                )
+            )
+    for first, _ in pieces:
+        first.start()
+    for first, second in pieces:
+        first.wait()
+        second.start()
+    for _, second in pieces:
+        second.wait()
 
 
 def sds(shape, dtype):
@@ -430,19 +514,24 @@
     square = pltpu.VMEM((2, BLOCK, BLOCK), F32)
     transfers = [pltpu.VMEM(shape, BF16) for _ in range(4) for shape in (small, large)]
     edges = [pltpu.VMEM((CHUNKS, CHUNK, STATE), F32)] * 2
-    layer_out, grad_x, grad_w, grad_r, grad_s, params = pl.pallas_call(
+    results = (
+        sds((ROWS, WIDTH), BF16),
+        sds((ROWS, WIDTH), BF16),
+        sds((ROWS, STATE), BF16),
+        sds((ROWS, STATE), BF16),
+        sds((HEADS, ROWS), BF16),
+        sds((3, HEADS), F32),
+    )
+    found = pl.pallas_call(
         layer_kernel,
-        out_shape=(
-            sds((ROWS, WIDTH), BF16),
-            sds((ROWS, WIDTH), BF16),
-            sds((ROWS, STATE), BF16),
-            sds((ROWS, STATE), BF16),
-            sds((HEADS, ROWS), BF16),
-            sds((1, 128), F32),
-        ),
+        out_shape=results,
         in_specs=[pl.BlockSpec(memory_space=pltpu.SMEM)] + vmem(10),
         out_specs=tuple(vmem(6)),
         scratch_shapes=[
+            *[pltpu.VMEM((PEERS, QUART, 128), BF16)] * 4,
+            pltpu.VMEM((1, 1, 128), F32),
+            pltpu.VMEM((PEERS, 1, 128), F32),
+            pltpu.VMEM((PEERS, QUART, 128), F32),
             *transfers,
             *edges,
             pltpu.VMEM((SLOTS, ROWS), BF16),
@@ -470,10 +559,10 @@
             per_head,
             per_head,
             pltpu.VMEM((ROWS, 2 * STATE), BF16),
-            pltpu.SemaphoreType.DMA((CHUNKS + 1,)),
-            pltpu.SemaphoreType.DMA((CHUNKS + 1,)),
-            pltpu.SemaphoreType.DMA((CHUNKS + 1,)),
-            pltpu.SemaphoreType.DMA((CHUNKS + 1,)),
+            pltpu.SemaphoreType.DMA((CHUNKS + 3,)),
+            pltpu.SemaphoreType.DMA((CHUNKS + 3,)),
+            pltpu.SemaphoreType.DMA((CHUNKS + 3,)),
+            pltpu.SemaphoreType.DMA((CHUNKS + 3,)),
             pltpu.SemaphoreType.DMA((CHUNKS,)),
             pltpu.SemaphoreType.DMA((CHUNKS,)),
         ],
@@ -486,7 +575,17 @@
         head_inputs, write_vecs, read_vecs, step_raw.T, out_cotangent,
         decay_log.reshape(1, HEADS), step_bias.reshape(1, HEADS), skip_gain.reshape(1, HEADS),
     )
-    return (layer_out, grad_x, grad_w, grad_r, grad_s.T, params[0, HEADS:].reshape(3, HEADS))
+    moved = pl.pallas_call(
+        finish_kernel,
+        out_shape=results[:5],
+        in_specs=[pl.BlockSpec(memory_space=pl.ANY)] * 5,
+        out_specs=tuple([pl.BlockSpec(memory_space=pl.ANY)] * 5),
+        scratch_shapes=[pltpu.VMEM(r.shape, r.dtype) for r in results[:5]]
+        + [pltpu.SemaphoreType.DMA((11,))] * 2,
+        name="finish",
+    )(*found[:5])
+    layer_out, grad_x, grad_w, grad_r, grad_s = moved
+    return (layer_out, grad_x, grad_w, grad_r, grad_s.T, found[5])
 
 
 def solution(mesh):

time: 265 us -> 254 us (0.958); the launches traced: 262 us -> 254 us
  local copies, waits for them, and re-layouts: 8.02 us -> 0.58 us
    unnamed x13 -> x3, local copies, waits for them, and re-layouts: 6.66 us -> 0.58 us
    pallas_call x1 -> x2, Pallas kernels: 254 us -> 253 us  [the longest x1 249 us: per_device(): pl.pallas_call(layer_kernel, out_shape=results, in_specs=[pl.BlockSpec(me...]
where the time goes in v2:
time: 254 us
  Pallas kernels  253 us (100%)
    pallas_call x1, Pallas kernels, per_device(): pl.pallas_call(layer_kernel, out_shape=results, in_specs=[pl.BlockSpec(me...  249 us

profile of v2, /device:TPU:1, one launch (start us, length us, event | category | flops | bytes accessed | tf_op | source)
XLA Modules:
  0.0 254.4 jit_solution(1432698039327017317)
XLA Ops:
  0.6 249.1 %layer.1 = (bf16[512,2048]{1,0:T(8,128)(2,1)}, bf16[512,2048]{1,0:T(8,128)(2,1)}, bf16[512,256]{1,0:T(8,128)(2,1)}, bf16[512,256]{1,0:T(8,128)(2,1)}, bf16[32,512]{1,0:T(8,128)(2,1)}, /*index=5*/f32[3,32]{1,0:T(4,128)}) custom-call(s32[1,3]{1,0:T(1,128)} %len_ref.1, s32[1,512]{1,0:T(1,128)} %bitcast.8, s32[1,512]{1,0:T(1,128)} %bitcast.9, ...), custom_call_target="tpu_custom_call" | custom-call | tf_op jit(solution)/shard_map/layer/pallas_call | solution.py:525
  249.7 0.0 copy-start
  249.7 4.1 %finish.1 = (bf16[512,2048]{1,0:T(8,128)(2,1)}, bf16[512,2048]{1,0:T(8,128)(2,1)}, bf16[512,256]{1,0:T(8,128)(2,1)}, bf16[512,256]{1,0:T(8,128)(2,1)}, bf16[32,512]{1,0:T(8,128)(2,1)}) custom-call(bf16[512,2048]{1,0:T(8,128)(2,1)} %get-tuple-element.17.refs_0_, bf16[512,2048]{1,0:T(8,128)(2,1)} %get-tuple-element.18.refs_1_, ...), custom_call_target="tpu_custom_call" | custom-call | tf_op jit(solution)/shard_map/finish/pallas_call | solution.py:578
  253.8 0.0 copy-done
  253.8 0.6 copy.18
Async XLA Ops:
  249.7 4.1 %copy-start = (f32[3,32]{1,0:T(4,128)S(1)}, f32[3,32]{1,0:T(4,128)}, u32[]{:S(2)}) copy-start(f32[3,32]{1,0:T(4,128)} %get-tuple-element.39) | copy-start | bytes 1156

commit v3 on v2

--- a/solution.py
+++ b/solution.py
@@ -129,10 +129,16 @@
     return nn(rate, upto, precision=PRECISE)
 
 
+def peer_number(me, k):
+    odd = lax.rem(k, 2)
+    offset = odd * ((k + 1) // 2) + (1 - odd) * (PEERS - k // 2)
+    return lax.rem(me + offset, PEERS)
+
+
 def peer_copies(me, source, target, send_sem, recv_sem):
     @pl.loop(1, PEERS)
     def _(k):
-        peer = lax.rem(me + k, PEERS)
+        peer = peer_number(me, k)
         pltpu.make_async_remote_copy(
             src_ref=source.at[pl.ds(pl.multiple_of(peer * CAP, CAP), CAP)],
             dst_ref=target.at[pl.ds(pl.multiple_of(me * CAP, CAP), CAP)],
@@ -151,7 +157,7 @@
 
     @pl.loop(1, PEERS)
     def _(k):
-        peer = lax.rem(me + k, PEERS)
+        peer = peer_number(me, k)
         pltpu.make_async_remote_copy(
             src_ref=source.at[0 if single else peer],
             dst_ref=target.at[me],

time: 254 us -> 255 us (level)
  no operation moved by 1% of the time
where the time goes in v3:
time: 255 us
  Pallas kernels  254 us (100%)
    pallas_call x1, Pallas kernels, per_device(): pl.pallas_call(layer_kernel, out_shape=results, in_specs=[pl.BlockSpec(me...  250 us

profile of v3, /device:TPU:1, one launch (start us, length us, event | category | flops | bytes accessed | tf_op | source)
XLA Modules:
  0.0 255.0 jit_solution(6880436735178814957)
XLA Ops:
  0.6 249.7 %layer.1 = (bf16[512,2048]{1,0:T(8,128)(2,1)}, bf16[512,2048]{1,0:T(8,128)(2,1)}, bf16[512,256]{1,0:T(8,128)(2,1)}, bf16[512,256]{1,0:T(8,128)(2,1)}, bf16[32,512]{1,0:T(8,128)(2,1)}, /*index=5*/f32[3,32]{1,0:T(4,128)}) custom-call(s32[1,3]{1,0:T(1,128)} %len_ref.1, s32[1,512]{1,0:T(1,128)} %bitcast.8, s32[1,512]{1,0:T(1,128)} %bitcast.9, ...), custom_call_target="tpu_custom_call" | custom-call | tf_op jit(solution)/shard_map/layer/pallas_call | solution.py:531
  250.3 0.0 copy-start
  250.4 4.1 %finish.1 = (bf16[512,2048]{1,0:T(8,128)(2,1)}, bf16[512,2048]{1,0:T(8,128)(2,1)}, bf16[512,256]{1,0:T(8,128)(2,1)}, bf16[512,256]{1,0:T(8,128)(2,1)}, bf16[32,512]{1,0:T(8,128)(2,1)}) custom-call(bf16[512,2048]{1,0:T(8,128)(2,1)} %get-tuple-element.17.refs_0_, bf16[512,2048]{1,0:T(8,128)(2,1)} %get-tuple-element.18.refs_1_, ...), custom_call_target="tpu_custom_call" | custom-call | tf_op jit(solution)/shard_map/finish/pallas_call | solution.py:584
  254.4 0.0 copy-done
  254.5 0.6 copy.18
Async XLA Ops:
  250.3 4.1 %copy-start = (f32[3,32]{1,0:T(4,128)S(1)}, f32[3,32]{1,0:T(4,128)}, u32[]{:S(2)}) copy-start(f32[3,32]{1,0:T(4,128)} %get-tuple-element.39) | copy-start | bytes 1156
